TPU v7x, 256 devices: a whole 4x4x8 slice. The times are simulated.
256 devices in a mesh: chan: 32 (over y_hi, z, core), day: 8 (over y_lo, x).
Axes of the slice: x: 4, y: 4 (y_hi: 2, y_lo: 2; y = y_hi * 2 + y_lo), z: 8, core: 2. Of those that a mesh axis runs over, the one named last changes fastest.
Arguments:
- spectra: bfloat16 [8, 512, 80, 256], P('day', 'chan'), may hold values from -500 to 500
Outputs:
- stacked: float32 [512, 512, 256], P('day', 'chan')
All inputs are finite; a program needn't handle non-finite values.
Results may differ from a plain program's by a relative error of at most 0.0023.
Values may be sent and summed in bfloat16 or wider, within the bound.
A program may use at most 128 MiB of HBM per device.

v0:
```python
import jax
import jax.numpy as jnp
from jax import lax
from jax.sharding import PartitionSpec as P


def freq_taper(bins):
    freq_index = jnp.arange(bins, dtype=jnp.float32)
    half_taper = 0.54 - 0.46 * jnp.cos(2.0 * jnp.pi * (freq_index + 0.5) / bins)
    return jnp.concatenate([half_taper, half_taper])


def whiten(spectra):
    values = spectra.astype(jnp.float32)
    bins = values.shape[-1] // 2
    band_power = jnp.sum(values * values, axis=-1, keepdims=True) / bins + 1e-06
    return (values * freq_taper(bins) / jnp.sqrt(band_power)).astype(jnp.bfloat16)


def lag_matrix(bins):
    lag_count = 2 * bins
    freq_index = jnp.arange(bins, dtype=jnp.int32)
    lag_index = jnp.arange(lag_count, dtype=jnp.int32) - bins
    wound = jnp.mod(freq_index[:, None] * lag_index[None, :], lag_count)
    phase_angle = 2.0 * jnp.pi / lag_count * wound.astype(jnp.float32)
    return jnp.concatenate([jnp.cos(phase_angle), -jnp.sin(phase_angle)], axis=0)


def cross_spectra(far_rows, near_rows):
    bins = far_rows.shape[-1] // 2
    windows = far_rows.shape[-2]
    far_re, far_im = (far_rows[..., :bins], far_rows[..., bins:])
    near_re, near_im = (near_rows[..., :bins], near_rows[..., bins:])
    real_part = jnp.einsum("jwf,iwf->jif", far_re, near_re, preferred_element_type=jnp.float32)
    real_part = real_part + jnp.einsum(
        "jwf,iwf->jif", far_im, near_im, preferred_element_type=jnp.float32
    )
    imag_part = jnp.einsum("jwf,iwf->jif", far_re, near_im, preferred_element_type=jnp.float32)
    imag_part = imag_part - jnp.einsum(
        "jwf,iwf->jif", far_im, near_re, preferred_element_type=jnp.float32
    )
    return jnp.concatenate([real_part, imag_part], axis=-1) / windows


def to_lags(cross, table):
    flat = cross.reshape(-1, cross.shape[-1])
    lagged = jnp.dot(
        flat, table, precision=lax.Precision.HIGHEST, preferred_element_type=jnp.float32
    )
    return lagged.reshape(cross.shape[:-1] + (table.shape[1],))


def shards(spectra):
    local_white = whiten(spectra)[0]
    gathered = lax.all_gather(local_white, "chan", axis=0, tiled=True)
    table = lag_matrix(local_white.shape[-1] // 2)
    day_count = lax.axis_size("day")
    return lax.psum_scatter(
        to_lags(cross_spectra(gathered, local_white), table) / day_count,
        "day",
        scatter_dimension=0,
        tiled=True,
    )


def solution(mesh):
    placed = (P("day", "chan", None, None),)
    return jax.shard_map(
        shards, mesh=mesh, in_specs=placed, out_specs=P("day", "chan", None), check_vma=False
    )
```

profile of v0, /device:TPU:1, one launch (start us, length us, event | category | flops | bytes accessed | tf_op | source)
XLA Modules:
  0.0 388.7 jit_solution(6104578910609152110)
XLA Ops:
  6.5 0.0 all-gather.3.cloned.1.call-start
  6.6 1.4 fusion.6
  8.1 2.2 fusion.5
  10.2 0.0 all-gather.3.cloned.1.call-update
  10.2 0.0 reduce-scatter.2.cloned.1.call-start
  10.3 1.3 fusion.32
  11.6 0.1 fusion.19
  11.8 0.4 copy.8
  12.2 0.4 copy.5
  12.6 0.5 fusion.15
  13.2 160.3 %all-gather.3.cloned.1.call-done = bf16[1,512,80,256]{3,2,0,1:T(8,128)(2,1)} async-done(((bf16[1,16,80,256]{3,2,0,1:T(8,128)(2,1)}), bf16[1,512,80,256]{3,2,0,1:T(8,128)(2,1)}) %all-gather.3.cloned.1.call-update) | async-done | bytes 20971536 | tf_op jit(solution)/shard_map/all_gather | solution.py:55
  173.5 17.1 %fusion.18 = (bf16[512,80,128]{2,1,0:T(8,128)(2,1)}, bf16[512,80,128]{2,1,0:T(8,128)(2,1)}) fusion(bf16[512,80,256]{2,1,0:T(8,128)(2,1)} %bitcast.23), kind=kLoop, calls=%fused_computation.33 | loop fusion | bytes 41943040 | tf_op jit(solution)/shard_map/slice | solution.py:32
  190.6 17.4 %copy.9 = bf16[512,80,128]{0,1,2:T(8,128)(2,1)} copy(bf16[512,80,128]{2,1,0:T(8,128)(2,1)} %get-tuple-element.5) | data formatting | bytes 20971520 | tf_op jit(solution)/shard_map/slice | solution.py:32
  208.0 0.0 copy-start.1
  208.0 7.6 %fusion.21 = f32[128,16,512]{2,1,0:T(8,128)} fusion(bf16[16,80,128]{1,0,2:T(8,128)(2,1)S(1)} %copy.8, bf16[512,80,128]{0,1,2:T(8,128)(2,1)} %copy.9), kind=kOutput, calls=%fused_computation.36 | convolution fusion | flops 167772160 | bytes 15007744 | tf_op jit(solution)/shard_map/jwf,iwf->jif/dot_general | solution.py:35
  215.6 0.2 copy-done.1
  215.8 2.9 fusion.23
  218.7 17.4 %copy.6 = bf16[512,80,128]{0,1,2:T(8,128)(2,1)} copy(bf16[512,80,128]{2,1,0:T(8,128)(2,1)} %get-tuple-element.6) | data formatting | bytes 20971520 | tf_op jit(solution)/shard_map/slice | solution.py:32
  236.1 0.0 copy-start
  236.1 7.6 %fusion.20 = f32[128,16,512]{2,1,0:T(8,128)} fusion(bf16[16,80,128]{1,0,2:T(8,128)(2,1)S(1)} %copy.5, bf16[512,80,128]{0,1,2:T(8,128)(2,1)} %copy.6), kind=kOutput, calls=%fused_computation.35 | convolution fusion | flops 167772160 | bytes 15007744 | tf_op jit(solution)/shard_map/jwf,iwf->jif/dot_general | solution.py:34
  243.7 0.2 copy-done
  243.8 2.9 fusion.22
  246.8 5.3 %copy.10 = f32[128,16,512]{0,2,1:T(8,128)} copy(f32[128,16,512]{2,1,0:T(8,128)} %fusion.21) | data formatting | bytes 8388608 | tf_op jit(solution)/shard_map/jwf,iwf->jif/dot_general | solution.py:35
  252.1 5.3 %copy.12 = f32[128,16,512]{0,2,1:T(8,128)} copy(f32[128,16,512]{2,1,0:T(8,128)} %fusion.23) | data formatting | bytes 8388608 | tf_op jit(solution)/shard_map/jwf,iwf->jif/dot_general | solution.py:39
  257.4 5.3 %copy.7 = f32[128,16,512]{0,2,1:T(8,128)} copy(f32[128,16,512]{2,1,0:T(8,128)} %fusion.20) | data formatting | bytes 8388608 | tf_op jit(solution)/shard_map/jwf,iwf->jif/dot_general | solution.py:34
  262.7 5.3 %copy.11 = f32[128,16,512]{0,2,1:T(8,128)} copy(f32[128,16,512]{2,1,0:T(8,128)} %fusion.22) | data formatting | bytes 8388608 | tf_op jit(solution)/shard_map/jwf,iwf->jif/dot_general | solution.py:38
  268.0 8.9 %subtract_bitcast_fusion = (f32[512,16,128]{2,0,1:T(8,128)S(1)}, f32[512,16,128]{2,0,1:T(8,128)}) fusion(f32[128,16,512]{0,2,1:T(8,128)} %copy.11, f32[128,16,512]{0,2,1:T(8,128)} %copy.12, f32[128,16,512]{0,2,1:T(8,128)} %copy.7, f32[128,16,512]{0,2,1:T(8,128)} %copy.10), kind=kLoop, calls=%fused_computation.6 | loop fusion | flops 2097152 | bytes 25165824 | tf_op jit(solution)/shard_map/sub | solution.py:39
  276.9 10.5 %broadcast_multiply_fusion = f32[512,16,256]{2,0,1:T(8,128)} fusion(f32[512,16,128]{2,0,1:T(8,128)S(1)} %get-tuple-element.11, f32[512,16,128]{2,0,1:T(8,128)} %get-tuple-element.12, f32[128,256]{1,0:T(8,128)S(1)} %get-tuple-element.10, f32[128,256]{1,0:T(8,128)S(1)} %get-tuple-element.9), kind=kOutput, calls=%fused_computation.4 | convolution fusion | flops 6448807936 | bytes 17039360 | tf_op jit(solution)/shard_map/dot_general | solution.py:47
  287.4 0.0 reduce-scatter.2.cloned.1.call-update
  287.4 91.7 %reduce-scatter.2.cloned.1.call-done = f32[64,16,256]{2,0,1:T(8,128)} async-done(((f32[512,16,256]{2,0,1:T(8,128)}), f32[64,16,256]{2,0,1:T(8,128)}) %reduce-scatter.2.cloned.1.call-update) | async-done | bytes 1048592 | tf_op jit(solution)/shard_map/reduce_scatter | solution.py:58
  379.1 2.8 copy.4
  (4 shorter events, 0.1 us)
Async XLA Ops:
  6.5 166.9 %all-gather.3.cloned.1.call-start = ((), (), s32[]{:S(2)}) async-start(), calls=%async_computation.2 | async-start | bytes 21626880 | tf_op jit(solution)/shard_map/all_gather | solution.py:55
  10.2 368.8 %reduce-scatter.2.cloned.1.call-start = ((), (), s32[]{:S(2)}) async-start(), calls=%async_computation.1 | async-start | bytes 9437184 | tf_op jit(solution)/shard_map/reduce_scatter | solution.py:58
  208.0 7.8 %copy-start.1 = (bf16[512,80,128]{0,1,2:T(8,128)(2,1)S(1)}, bf16[512,80,128]{0,1,2:T(8,128)(2,1)}, u32[]{:S(2)}) copy-start(bf16[512,80,128]{0,1,2:T(8,128)(2,1)} %copy.9) | copy-start | bytes 31457284
  236.1 7.8 %copy-start = (bf16[512,80,128]{0,1,2:T(8,128)(2,1)S(1)}, bf16[512,80,128]{0,1,2:T(8,128)(2,1)}, u32[]{:S(2)}) copy-start(bf16[512,80,128]{0,1,2:T(8,128)(2,1)} %copy.6) | copy-start | bytes 31457284
Sparse Core Ops, SparseCore 0:
  10.4 163.0 all-gather.2
  287.5 91.4 reduce-scatter.1
where the time goes:
time: 390 us; the launch traced here: 389 us
  waiting for transfers between devices  252 us (65%)
  local copies, waits for them, and re-layouts  77.2 us (20%)
  matrix products  31.6 us (8%)
  other arithmetic  14.4 us (4%)
  between operations  13.5 us (3%)
    all_gather x1, waiting for transfers between devices, shards(): gathered = lax.all_gather(local_white, 'chan', axis=0, tiled=True)  160 us
    reduce_scatter x1, waiting for transfers between devices, shards(): lax.psum_scatter(to_lags(cross_spectra(gathered, local_white), table) / d...  91.7 us
    slice x3, local copies, waits for them, and re-layouts, cross_spectra(): far_re, far_im = (far_rows[..., :bins], far_rows[..., bins:])  51.9 us
    dot_general x1, matrix products, to_lags(): jnp.dot(flat, table, precision=lax.Precision.HIGHEST, preferred_element_t...  10.5 us
    sub x1, other arithmetic, cross_spectra(): imag_part - jnp.einsum('jwf,iwf->jif', far_im, near_re, preferred_element...  8.86 us
  transfers between devices with their start and end apart: 2, of which 2 were waited for; matrix products, arithmetic and copies ran while one was open for 1% of the time, Pallas kernels for 0%

commit v1 on v0

v1 whole, which is shorter than its diff:
```python
import jax
import jax.numpy as jnp
import numpy as np
from jax import lax
from jax.experimental import pallas as pl
from jax.experimental.pallas import tpu as pltpu
from jax.sharding import PartitionSpec as P

F32 = jnp.float32
BF16 = jnp.bfloat16
MESH = pl.DeviceIdType.MESH
BINS = 128
LAGS = 256
WINDOWS = 80
CH = 16
DAYS = 8
CHIPS = 16
HEAD = 64
KB = 10
NT = (((1,), (1,)), ((), ()))


def taper_table():
    f = np.arange(BINS, dtype=np.float64)
    taper = 0.54 - 0.46 * np.cos(2.0 * np.pi * (f + 0.5) / BINS)
    return np.ascontiguousarray(np.broadcast_to(taper[:, None], (BINS, 128)).astype(np.float32))


def lag_tables():
    slot = np.arange(BINS)
    chip = slot % CHIPS
    f = (slot // CHIPS) * CHIPS + (chip % 4) * 4 + chip // 4
    wound = (f[:, None] * (np.arange(LAGS)[None, :] - BINS)) % LAGS
    angle = 2.0 * np.pi / LAGS * wound
    table = np.concatenate([np.cos(angle), -np.sin(angle)], axis=0) / (WINDOWS * DAYS)
    table = table.astype(np.float32)
    high = table.astype(jnp.bfloat16)
    low = (table - high.astype(np.float32)).astype(jnp.bfloat16)
    return high, low


def kernel(
    x_ref, taper_ref, high_ref, low_ref, out_ref,
    head_f, tail_f, send_a, recv_a, mix_f, send_b, recv_b, near, far,
    send_c, recv_c, recv_d, lag_f, lag_rows,
    a_send, a_recv, b_send, b_recv, s_send, s_recv, c_send, c_recv, d_send, d_recv,
):
    c = lax.axis_index("chan")
    d = lax.axis_index("day")
    core = lax.rem(c, 2)
    chip = c // 2
    chip_lo = lax.rem(chip, 4)
    chip_hi = chip // 4

    barrier = pltpu.get_barrier_semaphore()
    for e in range(1, DAYS):
        pl.semaphore_signal(barrier, inc=1, device_id={"day": d ^ e}, device_id_type=MESH)
    for m in range(1, CHIPS):
        pl.semaphore_signal(barrier, inc=1, device_id={"chan": c ^ (2 * m)}, device_id_type=MESH)
    pl.semaphore_signal(barrier, inc=1, device_id={"chan": c ^ 1}, device_id_type=MESH)

    lane = lax.broadcasted_iota(jnp.int32, (1, 128), 1)
    group = lane // 32
    first16 = lax.rem(lane, 32) < 16
    sign64 = jnp.where(lane < 64, -1.0, 1.0).astype(F32)
    sign16 = jnp.where(first16, -1.0, 1.0).astype(F32)

    def swap16(v):
        return jnp.where(first16, pltpu.roll(v, 112, 1), pltpu.roll(v, 16, 1))

    def whiten(g, carry):
        taper = taper_ref[...]
        tails = []
        for u in range(4):
            ch = g * 4 + u
            v = x_ref[0, ch].astype(F32)
            t = jnp.concatenate([v[:HEAD, :128], v[:HEAD, 128:]], axis=0).T
            part = jnp.sum(t * t, axis=0, keepdims=True)
            power = (part + pltpu.roll(part, 64, 1)) / BINS + 1e-06
            head_f[pl.ds(ch, 128, stride=CH), :] = t * taper * (1.0 / jnp.sqrt(power))
            tails += [v[HEAD:, :128], v[HEAD:, 128:]]
        t = jnp.concatenate(tails, axis=0).T
        part = jnp.sum(t * t, axis=0, keepdims=True)
        power = (part + swap16(part)) / BINS + 1e-06
        tail_f[pl.ds(g, 128, stride=4), :] = t * taper * (1.0 / jnp.sqrt(power))
        return carry

    lax.fori_loop(0, 4, whiten, 0)

    def pack(b, carry):
        send_a[b, 0:64, :] = head_f[pl.ds(pl.multiple_of(b * 64, 64), 64), :].astype(BF16)
        send_a[b, 64:80, :] = tail_f[pl.ds(pl.multiple_of(b * 16, 16), 16), :].astype(BF16)
        return carry

    lax.fori_loop(0, 32, pack, 0)

    pl.semaphore_wait(barrier, 23)

    for s in range(4):
        q = chip_lo ^ s
        for e in range(1, DAYS):
            to = d ^ e
            pltpu.make_async_remote_copy(
                send_a.at[to * 4 + q], recv_a.at[q, d], a_send, a_recv.at[s],
                device_id={"day": to}, device_id_type=MESH,
            ).start()
    for s in range(4):
        q = chip_lo ^ s
        recv_a[q, d] = send_a[d * 4 + q]

    def forward(src):
        return pltpu.make_async_remote_copy(
            recv_b.at[core, src], recv_b.at[core, src], s_send, s_recv.at[src],
            device_id={"chan": c ^ 1}, device_id_type=MESH,
        )

    def spread(side, src, mine):
        row = pl.multiple_of((src // 2) * 128 + lax.rem(src, 2) * 32 + side * 16, 16)
        for k in range(KB):
            z = recv_b[side, src, k]
            zf = z.astype(F32)
            turned = pltpu.roll(zf, 64, 1) * sign64 if k < DAYS else swap16(zf) * sign16
            far[pl.ds(row, 16), k * 128 : (k + 1) * 128] = z
            far[pl.ds(row + 64, 16), k * 128 : (k + 1) * 128] = turned.astype(BF16)
            if mine:
                near[pl.ds(pl.multiple_of(src * 16, 16), 16), k * 128 : (k + 1) * 128] = z

    for s in range(4):
        q = chip_lo ^ s
        pltpu.make_async_copy(
            recv_a.at[q, pl.ds(0, 7)], recv_a.at[q, pl.ds(0, 7)], a_recv.at[s]
        ).wait()
        for h in range(2):
            tiles = [recv_a[q, 4 * h + n, 64:80, :].astype(F32) for n in range(4)]
            for u in range(4):
                mixed = tiles[u]
                for n in range(4):
                    if n != u:
                        moved = pltpu.roll(tiles[n], (32 * (n - u)) % 128, 1)
                        mixed = jnp.where(group == n, moved, mixed)
                mix_f[pl.ds(h * 64 + u, 16, stride=4), :] = mixed
        for jj in range(4):
            j = chip_hi ^ jj
            to = 4 * j + q
            rows = pl.ds(pl.multiple_of(j * 16, 16), 16)
            tail_rows = [pl.ds(pl.multiple_of(h * 64 + j * 16, 16), 16) for h in range(2)]
            if s == 0 and jj == 0:
                recv_b[core, chip, 0:8] = recv_a[q, :, rows, :]
                for h in range(2):
                    recv_b[core, chip, 8 + h] = mix_f[tail_rows[h], :].astype(BF16)
                forward(chip).start()
            else:
                send_b[to, 0:8] = recv_a[q, :, rows, :]
                for h in range(2):
                    send_b[to, 8 + h] = mix_f[tail_rows[h], :].astype(BF16)
                pltpu.make_async_remote_copy(
                    send_b.at[to], recv_b.at[core, chip], b_send, b_recv.at[chip],
                    device_id={"chan": to * 2 + core}, device_id_type=MESH,
                ).start()

    spread(core, chip, True)

    def arrive(n, carry):
        src = chip ^ (lax.rem(n, 4) * 4 + n // 4)
        pltpu.make_async_copy(recv_b.at[core, src], recv_b.at[core, src], b_recv.at[src]).wait()
        forward(src).start()
        spread(core, src, True)
        return carry

    lax.fori_loop(1, CHIPS, arrive, 0)

    def arrive_other(n, carry):
        src = chip ^ (lax.rem(n, 4) * 4 + n // 4)
        side = 1 - core
        pltpu.make_async_copy(recv_b.at[side, src], recv_b.at[side, src], s_recv.at[src]).wait()
        spread(side, src, False)
        return carry

    lax.fori_loop(0, CHIPS, arrive_other, 0)

    for s in range(4):
        p = (d // 2) ^ s
        prod = lax.dot_general(
            near[...], far[pl.ds(pl.multiple_of(p * 256, 256), 256), :], NT,
            preferred_element_type=F32,
        )
        for e in range(2):
            send_c[2 * p + e] = prod[:, e * 128 : (e + 1) * 128].astype(BF16).reshape(CHIPS, 16, 128)
        recv_c[pl.ds(2 * p, 2), chip] = send_c[pl.ds(2 * p, 2), chip]
        for m in range(1, CHIPS):
            to = chip ^ m
            pltpu.make_async_remote_copy(
                send_c.at[pl.ds(2 * p, 2), to], recv_c.at[pl.ds(2 * p, 2), chip],
                c_send.at[s], c_recv.at[s],
                device_id={"chan": to * 2 + core}, device_id_type=MESH,
            ).start()

    for s in range(4):
        some = recv_c.at[pl.ds(0, 2), pl.ds(0, 15)]
        pltpu.make_async_copy(some, some, c_recv.at[s]).wait()
        for e in range(2):
            to = d ^ (2 * s + e)
            if s == 0 and e == 0:
                lag_f[pl.ds(pl.multiple_of(d * 256, 256), 256), :] = (
                    recv_c[d].reshape(256, 128).astype(F32)
                )
            else:
                pltpu.make_async_remote_copy(
                    recv_c.at[to], recv_d.at[d], d_send, d_recv.at[d],
                    device_id={"day": to}, device_id_type=MESH,
                ).start()
    for e in range(1, DAYS):
        src = d ^ e
        pltpu.make_async_copy(recv_d.at[src], recv_d.at[src], d_recv.at[src]).wait()
        lag_f[pl.ds(pl.multiple_of(src * 256, 256), 256), :] = (
            recv_d[src].reshape(256, 128).astype(F32)
        )

    for n in range(4):
        for u in range(4):
            t = lag_f[pl.ds(n * 4 + u, 128, stride=16), :].T.astype(BF16)
            lag_rows[u * 64 : (u + 1) * 64, 0:128] = t[0:64]
            lag_rows[u * 64 : (u + 1) * 64, 128:256] = t[64:128]
        rows = lag_rows[...]
        lags = jnp.dot(rows, high_ref[...], preferred_element_type=F32)
        lags = lags + jnp.dot(rows, low_ref[...], preferred_element_type=F32)
        for u in range(4):
            for h in range(2):
                out_ref[pl.ds((n * 4 + u) * 2 + h, 64, stride=32), :] = (
                    lags[u * 64 : (u + 1) * 64, h * 128 : (h + 1) * 128]
                )

    sent = send_a.at[pl.ds(0, 28)]
    pltpu.make_async_copy(sent, sent, a_send).wait()
    sent = send_b.at[pl.ds(0, 15)]
    pltpu.make_async_copy(sent, sent, b_send).wait()
    sent = recv_b.at[0]
    pltpu.make_async_copy(sent, sent, s_send).wait()
    for s in range(4):
        sent = send_c.at[pl.ds(0, 2), pl.ds(0, 15)]
        pltpu.make_async_copy(sent, sent, c_send.at[s]).wait()
    sent = recv_d.at[pl.ds(0, 7)]
    pltpu.make_async_copy(sent, sent, d_send).wait()


def shards(spectra):
    high, low = lag_tables()
    dma = pltpu.SemaphoreType.DMA
    out = pl.pallas_call(
        kernel,
        out_shape=jax.ShapeDtypeStruct((2048, 128), F32),
        in_specs=[pl.BlockSpec(memory_space=pltpu.VMEM)] * 4,
        out_specs=pl.BlockSpec(memory_space=pltpu.VMEM),
        scratch_shapes=[
            pltpu.VMEM((2048, 128), F32),
            pltpu.VMEM((512, 128), F32),
            pltpu.VMEM((32, 80, 128), BF16),
            pltpu.VMEM((4, 8, 80, 128), BF16),
            pltpu.VMEM((128, 128), F32),
            pltpu.VMEM((CHIPS, KB, 16, 128), BF16),
            pltpu.VMEM((2, CHIPS, KB, 16, 128), BF16),
            pltpu.VMEM((256, KB * 128), BF16),
            pltpu.VMEM((1024, KB * 128), BF16),
            pltpu.VMEM((DAYS, CHIPS, 16, 128), BF16),
            pltpu.VMEM((DAYS, CHIPS, 16, 128), BF16),
            pltpu.VMEM((DAYS, CHIPS, 16, 128), BF16),
            pltpu.VMEM((2048, 128), F32),
            pltpu.VMEM((256, 256), BF16),
            dma,
            dma((4,)),
            dma,
            dma((CHIPS,)),
            dma,
            dma((CHIPS,)),
            dma((4,)),
            dma((4,)),
            dma,
            dma((DAYS,)),
        ],
        compiler_params=pltpu.CompilerParams(
            collective_id=0, has_side_effects=True, vmem_limit_bytes=40 << 20
        ),
    )(spectra, jnp.asarray(taper_table()), jnp.asarray(high), jnp.asarray(low))
    return out.reshape(64, 16, 256)


def solution(mesh):
    return jax.shard_map(
        shards,
        mesh=mesh,
        in_specs=(P("day", "chan", None, None),),
        out_specs=P("day", "chan", None),
        check_vma=False,
    )
```

time: 390 us -> 61.5 us (0.16)
  waiting for transfers between devices: 252 us -> 0 us
  local copies, waits for them, and re-layouts: 77.2 us -> 5 us
  Pallas kernels: 0 us -> 56 us
  matrix products: 31.6 us -> 0 us
  other arithmetic: 14.4 us -> 0 us
  between operations: 13.5 us -> 0.01 us
    all_gather x1 -> x0, waiting for transfers between devices: 160 us -> none  [shards(): gathered = lax.all_gather(local_white, 'chan', axis=0, tiled=True)]
    reduce_scatter x1 -> x0, waiting for transfers between devices: 91.7 us -> none  [shards(): lax.psum_scatter(to_lags(cross_spectra(gathered, local_white), table) / d...]
    pallas_call x0 -> x1, Pallas kernels: none -> 56 us  [shards(): pl.pallas_call(kernel, out_shape=jax.ShapeDtypeStruct((2048, 128), F32),...]
    slice x6 -> x0, local copies, waits for them, and re-layouts: 52.8 us -> none  [the longest x3 51.9 us: cross_spectra(): far_re, far_im = (far_rows[..., :bins], far_rows[..., bins:])]
    dot_general x5 -> x0, matrix products: 31.6 us -> none  [the longest x1 10.5 us: to_lags(): jnp.dot(flat, table, precision=lax.Precision.HIGHEST, preferred_element_t...]
    dot_general x4 -> x0, local copies, waits for them, and re-layouts: 21.2 us -> none  [the longest x1 5.33 us: cross_spectra(): jnp.einsum('jwf,iwf->jif', far_im, near_re, preferred_element_type=jnp.fl...]
    sub x3 -> x0, other arithmetic: 8.91 us -> none  [the longest x1 8.86 us: cross_spectra(): imag_part - jnp.einsum('jwf,iwf->jif', far_im, near_re, preferred_element...]
  transfers between devices with their start and end apart: 2 -> 0, of which waited for: 2 -> 0; matrix products, arithmetic and copies ran while one was open for 1% -> 0% of each run, Pallas kernels for 0% -> 0%
where the time goes in v1:
time: 61.5 us; the launch traced here: 61 us
  Pallas kernels  56 us (91%)
  local copies, waits for them, and re-layouts  5 us (8%)
    pallas_call x1, Pallas kernels, shards(): pl.pallas_call(kernel, out_shape=jax.ShapeDtypeStruct((2048, 128), F32),...  56 us
    unnamed x8, local copies, waits for them, and re-layouts  3.73 us
    reshape x1, local copies, waits for them, and re-layouts, shards(): return out.reshape(64, 16, 256)  1.26 us

profile of v1, /device:TPU:1, one launch (start us, length us, event | category | flops | bytes accessed | tf_op | source)
XLA Modules:
  0.0 61.0 jit_solution(4898570710169280082)
XLA Ops:
  0.0 0.0 copy-start
  0.0 1.1 %copy-done = bf16[1,16,80,256]{3,2,1,0:T(8,128)(2,1)S(1)} copy-done((bf16[1,16,80,256]{3,2,1,0:T(8,128)(2,1)S(1)}, bf16[1,16,80,256]{3,2,1,0:T(8,128)(2,1)}, u32[]{:S(2)}) %copy-start) | copy-done | bytes 655384
  1.1 0.0 copy-start.1
  1.1 0.9 %copy-done.1 = bf16[256,256]{1,0:T(8,128)(2,1)S(1)} copy-done((bf16[256,256]{1,0:T(8,128)(2,1)S(1)}, bf16[256,256]{1,0:T(8,128)(2,1)}, u32[]{:S(2)}) %copy-start.1) | copy-done | bytes 131096
  2.0 0.0 copy-start.2
  2.0 0.9 %copy-done.2 = bf16[256,256]{1,0:T(8,128)(2,1)S(1)} copy-done((bf16[256,256]{1,0:T(8,128)(2,1)S(1)}, bf16[256,256]{1,0:T(8,128)(2,1)}, u32[]{:S(2)}) %copy-start.2) | copy-done | bytes 131096
  2.9 0.0 copy-start.3
  2.9 0.8 %copy-done.3 = f32[128,128]{1,0:T(8,128)S(1)} copy-done((f32[128,128]{1,0:T(8,128)S(1)}, f32[128,128]{1,0:T(8,128)}, u32[]{:S(2)}) %copy-start.3) | copy-done | bytes 65560
  3.7 56.0 %shard_map.46 = f32[2048,128]{1,0:T(8,128)S(1)} custom-call(bf16[1,16,80,256]{3,2,1,0:T(8,128)(2,1)S(1)} %copy-done, f32[128,128]{1,0:T(8,128)S(1)} %copy-done.3, bf16[256,256]{1,0:T(8,128)(2,1)S(1)} %copy-done.2, bf16[256,256]{1,0:T(8,128)(2,1)S(1)} %copy-done.1), custom_call_target="tpu_custom_call" | custom-call | tf_op jit(solution)/shard_map/pallas_call | solution.py:249
  59.8 1.3 %reshape.3 = f32[64,16,256]{2,1,0:T(8,128)} reshape(f32[2048,128]{1,0:T(8,128)S(1)} %shard_map.46) | data formatting | bytes 2097152 | tf_op jit(solution)/shard_map/reshape | solution.py:284
Async XLA Ops:
  0.0 1.1 %copy-start = (bf16[1,16,80,256]{3,2,1,0:T(8,128)(2,1)S(1)}, bf16[1,16,80,256]{3,2,1,0:T(8,128)(2,1)}, u32[]{:S(2)}) copy-start(bf16[1,16,80,256]{3,2,1,0:T(8,128)(2,1)} %x_ref.1) | copy-start | bytes 1966084
  1.1 0.9 %copy-start.1 = (bf16[256,256]{1,0:T(8,128)(2,1)S(1)}, bf16[256,256]{1,0:T(8,128)(2,1)}, u32[]{:S(2)}) copy-start(bf16[256,256]{1,0:T(8,128)(2,1)} %constant.8.clone.low_ref) | copy-start | bytes 393220
  2.0 0.9 %copy-start.2 = (bf16[256,256]{1,0:T(8,128)(2,1)S(1)}, bf16[256,256]{1,0:T(8,128)(2,1)}, u32[]{:S(2)}) copy-start(bf16[256,256]{1,0:T(8,128)(2,1)} %constant.7.clone.high_ref) | copy-start | bytes 393220
  2.9 0.8 %copy-start.3 = (f32[128,128]{1,0:T(8,128)S(1)}, f32[128,128]{1,0:T(8,128)}, u32[]{:S(2)}) copy-start(f32[128,128]{1,0:T(8,128)} %constant.6.clone.taper_ref) | copy-start | bytes 196612

commit v2 on v1

--- a/solution.py
+++ b/solution.py
@@ -40,10 +40,10 @@
 
 
 def kernel(
-    x_ref, taper_ref, high_ref, low_ref, out_ref,
-    head_f, tail_f, send_a, recv_a, mix_f, send_b, recv_b, near, far,
-    send_c, recv_c, recv_d, lag_f, lag_rows,
-    a_send, a_recv, b_send, b_recv, s_send, s_recv, c_send, c_recv, d_send, d_recv,
+    x_hbm, taper_hbm, tables_hbm, out_ref,
+    x_ref, taper_ref, tables, head_f, tail_f, send_a, recv_a, mix_f, send_b, recv_b, near, far,
+    send_c, recv_d, lag_f, lag_rows, out_f,
+    x_in, taper_in, tables_in,    a_send, a_recv, b_send, b_recv, s_send, s_recv, d_send, d_recv,
 ):
     c = lax.axis_index("chan")
     d = lax.axis_index("day")
@@ -52,6 +52,20 @@
     chip_lo = lax.rem(chip, 4)
     chip_hi = chip // 4
 
+    x_copies = [
+        pltpu.make_async_copy(
+            x_hbm.at[0, pl.ds(4 * g, 4)], x_ref.at[pl.ds(4 * g, 4)], x_in.at[g]
+        )
+        for g in range(4)
+    ]
+    taper_copy = pltpu.make_async_copy(taper_hbm, taper_ref, taper_in)
+    tables_copy = pltpu.make_async_copy(tables_hbm, tables, tables_in)
+    x_copies[0].start()
+    taper_copy.start()
+    for g in range(1, 4):
+        x_copies[g].start()
+    tables_copy.start()
+
     barrier = pltpu.get_barrier_semaphore()
     for e in range(1, DAYS):
         pl.semaphore_signal(barrier, inc=1, device_id={"day": d ^ e}, device_id_type=MESH)
@@ -68,12 +82,12 @@
     def swap16(v):
         return jnp.where(first16, pltpu.roll(v, 112, 1), pltpu.roll(v, 16, 1))
 
-    def whiten(g, carry):
+    def whiten(g):
         taper = taper_ref[...]
         tails = []
         for u in range(4):
             ch = g * 4 + u
-            v = x_ref[0, ch].astype(F32)
+            v = x_ref[ch].astype(F32)
             t = jnp.concatenate([v[:HEAD, :128], v[:HEAD, 128:]], axis=0).T
             part = jnp.sum(t * t, axis=0, keepdims=True)
             power = (part + pltpu.roll(part, 64, 1)) / BINS + 1e-06
@@ -83,9 +97,11 @@
         part = jnp.sum(t * t, axis=0, keepdims=True)
         power = (part + swap16(part)) / BINS + 1e-06
         tail_f[pl.ds(g, 128, stride=4), :] = t * taper * (1.0 / jnp.sqrt(power))
-        return carry
-
-    lax.fori_loop(0, 4, whiten, 0)
+
+    taper_copy.wait()
+    for g in range(4):
+        x_copies[g].wait()
+        whiten(g)
 
     def pack(b, carry):
         send_a[b, 0:64, :] = head_f[pl.ds(pl.multiple_of(b * 64, 64), 64), :].astype(BF16)
@@ -160,23 +176,24 @@
 
     spread(core, chip, True)
 
+    def at(n):
+        return chip ^ (lax.rem(n, 4) * 4 + n // 4)
+
+    def take_other(src):
+        side = 1 - core
+        pltpu.make_async_copy(recv_b.at[side, src], recv_b.at[side, src], s_recv.at[src]).wait()
+        spread(side, src, False)
+
     def arrive(n, carry):
-        src = chip ^ (lax.rem(n, 4) * 4 + n // 4)
+        src = at(n)
         pltpu.make_async_copy(recv_b.at[core, src], recv_b.at[core, src], b_recv.at[src]).wait()
         forward(src).start()
         spread(core, src, True)
+        take_other(at(n - 1))
         return carry
 
     lax.fori_loop(1, CHIPS, arrive, 0)
-
-    def arrive_other(n, carry):
-        src = chip ^ (lax.rem(n, 4) * 4 + n // 4)
-        side = 1 - core
-        pltpu.make_async_copy(recv_b.at[side, src], recv_b.at[side, src], s_recv.at[src]).wait()
-        spread(side, src, False)
-        return carry
-
-    lax.fori_loop(0, CHIPS, arrive_other, 0)
+    take_other(at(CHIPS - 1))
 
     for s in range(4):
         p = (d // 2) ^ s
@@ -186,49 +203,49 @@
         )
         for e in range(2):
             send_c[2 * p + e] = prod[:, e * 128 : (e + 1) * 128].astype(BF16).reshape(CHIPS, 16, 128)
-        recv_c[pl.ds(2 * p, 2), chip] = send_c[pl.ds(2 * p, 2), chip]
-        for m in range(1, CHIPS):
-            to = chip ^ m
+
+        def keep(day, to):
             pltpu.make_async_remote_copy(
-                send_c.at[pl.ds(2 * p, 2), to], recv_c.at[pl.ds(2 * p, 2), chip],
-                c_send.at[s], c_recv.at[s],
-                device_id={"chan": to * 2 + core}, device_id_type=MESH,
+                send_c.at[day, to], recv_d.at[d, chip], d_send, d_recv.at[d],
+                device_id={"chan": to * 2 + core, "day": day}, device_id_type=MESH,
             ).start()
 
-    for s in range(4):
-        some = recv_c.at[pl.ds(0, 2), pl.ds(0, 15)]
-        pltpu.make_async_copy(some, some, c_recv.at[s]).wait()
-        for e in range(2):
-            to = d ^ (2 * s + e)
-            if s == 0 and e == 0:
-                lag_f[pl.ds(pl.multiple_of(d * 256, 256), 256), :] = (
-                    recv_c[d].reshape(256, 128).astype(F32)
-                )
-            else:
-                pltpu.make_async_remote_copy(
-                    recv_c.at[to], recv_d.at[d], d_send, d_recv.at[d],
-                    device_id={"day": to}, device_id_type=MESH,
-                ).start()
-    for e in range(1, DAYS):
+        def keep_both(m, carry):
+            for e in range(2):
+                keep(d ^ (2 * s + e), chip ^ m)
+            return carry
+
+        lax.fori_loop(1, CHIPS, keep_both, 0)
+        keep(d ^ (2 * s + 1), chip)
+        if s == 0:
+            recv_d[d, chip] = send_c[d, chip]
+        else:
+            keep(d ^ (2 * s), chip)
+
+    for e in range(DAYS):
         src = d ^ e
-        pltpu.make_async_copy(recv_d.at[src], recv_d.at[src], d_recv.at[src]).wait()
+        some = recv_d.at[src] if e else recv_d.at[src, pl.ds(0, 15)]
+        pltpu.make_async_copy(some, some, d_recv.at[src]).wait()
         lag_f[pl.ds(pl.multiple_of(src * 256, 256), 256), :] = (
             recv_d[src].reshape(256, 128).astype(F32)
         )
 
+    tables_copy.wait()
     for n in range(4):
         for u in range(4):
             t = lag_f[pl.ds(n * 4 + u, 128, stride=16), :].T.astype(BF16)
             lag_rows[u * 64 : (u + 1) * 64, 0:128] = t[0:64]
             lag_rows[u * 64 : (u + 1) * 64, 128:256] = t[64:128]
         rows = lag_rows[...]
-        lags = jnp.dot(rows, high_ref[...], preferred_element_type=F32)
-        lags = lags + jnp.dot(rows, low_ref[...], preferred_element_type=F32)
+        lags = jnp.dot(rows, tables[0], preferred_element_type=F32)
+        lags = lags + jnp.dot(rows, tables[1], preferred_element_type=F32)
         for u in range(4):
             for h in range(2):
-                out_ref[pl.ds((n * 4 + u) * 2 + h, 64, stride=32), :] = (
+                out_f[h, pl.ds(n * 4 + u, 64, stride=16), :] = (
                     lags[u * 64 : (u + 1) * 64, h * 128 : (h + 1) * 128]
                 )
+    for h in range(2):
+        out_ref[:, h * 128 : (h + 1) * 128] = out_f[h]
 
     sent = send_a.at[pl.ds(0, 28)]
     pltpu.make_async_copy(sent, sent, a_send).wait()
@@ -236,22 +253,21 @@
     pltpu.make_async_copy(sent, sent, b_send).wait()
     sent = recv_b.at[0]
     pltpu.make_async_copy(sent, sent, s_send).wait()
-    for s in range(4):
-        sent = send_c.at[pl.ds(0, 2), pl.ds(0, 15)]
-        pltpu.make_async_copy(sent, sent, c_send.at[s]).wait()
-    sent = recv_d.at[pl.ds(0, 7)]
+    sent = send_c.reshape(128, 16, 128).at[pl.ds(0, 127)]
     pltpu.make_async_copy(sent, sent, d_send).wait()
 
 
 def shards(spectra):
-    high, low = lag_tables()
     dma = pltpu.SemaphoreType.DMA
     out = pl.pallas_call(
         kernel,
-        out_shape=jax.ShapeDtypeStruct((2048, 128), F32),
-        in_specs=[pl.BlockSpec(memory_space=pltpu.VMEM)] * 4,
+        out_shape=jax.ShapeDtypeStruct((1024, 256), F32),
+        in_specs=[pl.BlockSpec(memory_space=pltpu.HBM)] * 3,
         out_specs=pl.BlockSpec(memory_space=pltpu.VMEM),
         scratch_shapes=[
+            pltpu.VMEM((CH, WINDOWS, 2 * BINS), BF16),
+            pltpu.VMEM((BINS, 128), F32),
+            pltpu.VMEM((2, LAGS, LAGS), BF16),
             pltpu.VMEM((2048, 128), F32),
             pltpu.VMEM((512, 128), F32),
             pltpu.VMEM((32, 80, 128), BF16),
@@ -263,24 +279,25 @@
             pltpu.VMEM((1024, KB * 128), BF16),
             pltpu.VMEM((DAYS, CHIPS, 16, 128), BF16),
             pltpu.VMEM((DAYS, CHIPS, 16, 128), BF16),
-            pltpu.VMEM((DAYS, CHIPS, 16, 128), BF16),
             pltpu.VMEM((2048, 128), F32),
             pltpu.VMEM((256, 256), BF16),
-            dma,
+            pltpu.VMEM((2, 1024, 128), F32),
             dma((4,)),
             dma,
+            dma,
+            dma,
+            dma((4,)),
+            dma,
             dma((CHIPS,)),
             dma,
             dma((CHIPS,)),
-            dma((4,)),
-            dma((4,)),
             dma,
             dma((DAYS,)),
         ],
         compiler_params=pltpu.CompilerParams(
-            collective_id=0, has_side_effects=True, vmem_limit_bytes=40 << 20
+            collective_id=0, has_side_effects=True, vmem_limit_bytes=56 << 20
         ),
-    )(spectra, jnp.asarray(taper_table()), jnp.asarray(high), jnp.asarray(low))
+    )(spectra, jnp.asarray(taper_table()), jnp.asarray(np.stack(lag_tables())))
     return out.reshape(64, 16, 256)
 
 

time: 61.5 us -> 57.8 us (0.940)
  local copies, waits for them, and re-layouts: 5 us -> 2.26 us
    unnamed x8 -> x1, local copies, waits for them, and re-layouts: 3.73 us -> 2.26 us
    reshape x1 -> x0, local copies, waits for them, and re-layouts: 1.26 us -> none  [shards(): return out.reshape(64, 16, 256)]
    pallas_call x1, Pallas kernels: 56 us -> 55.4 us  [shards(): pl.pallas_call(kernel, out_shape=jax.ShapeDtypeStruct((1024, 256), F32),...]
where the time goes in v2:
time: 57.8 us; the launch traced here: 57.6 us
  Pallas kernels  55.4 us (96%)
  local copies, waits for them, and re-layouts  2.26 us (4%)
    pallas_call x1, Pallas kernels, shards(): pl.pallas_call(kernel, out_shape=jax.ShapeDtypeStruct((1024, 256), F32),...  55.4 us
    unnamed x1, local copies, waits for them, and re-layouts  2.26 us

profile of v2, /device:TPU:1, one launch (start us, length us, event | category | flops | bytes accessed | tf_op | source)
XLA Modules:
  0.0 57.6 jit_solution(8735341068687826428)
XLA Ops:
  0.0 55.4 %shard_map.37 = f32[1024,256]{1,0:T(8,128)} custom-call(bf16[1,16,80,256]{3,2,1,0:T(8,128)(2,1)} %x_hbm.1, f32[128,128]{1,0:T(8,128)} %constant.4.clone.taper_hbm, bf16[2,256,256]{2,1,0:T(8,128)(2,1)} %constant.5.clone.tables_hbm), custom_call_target="tpu_custom_call" | custom-call | tf_op jit(solution)/shard_map/pallas_call | solution.py:262
  55.4 2.3 %copy.5 = f32[64,16,256]{2,1,0:T(8,128)} copy(f32[64,16,256]{2,1,0:T(8,128)} %bitcast.1) | data formatting | bytes 2097152

commit v3 on v2

v3 whole, which is shorter than its diff:
```python
import jax
import jax.numpy as jnp
import numpy as np
from jax import lax
from jax.experimental import pallas as pl
from jax.experimental.pallas import tpu as pltpu
from jax.sharding import PartitionSpec as P

F32 = jnp.float32
BF16 = jnp.bfloat16
MESH = pl.DeviceIdType.MESH
BINS = 128
LAGS = 256
WINDOWS = 80
CH = 16
DAYS = 8
CHIPS = 16
HEAD = 64
KB = 10
NT = (((1,), (1,)), ((), ()))


def taper_table():
    f = np.arange(BINS, dtype=np.float64)
    taper = 0.54 - 0.46 * np.cos(2.0 * np.pi * (f + 0.5) / BINS)
    return np.ascontiguousarray(np.broadcast_to(taper[:, None], (BINS, 128)).astype(np.float32))


def lag_tables():
    slot = np.arange(BINS)
    day = slot // CHIPS
    f = (day % 4) * 32 + (day // 4) * 16 + slot % CHIPS
    wound = (f[:, None] * (np.arange(LAGS)[None, :] - BINS)) % LAGS
    angle = 2.0 * np.pi / LAGS * wound
    table = np.concatenate([np.cos(angle), -np.sin(angle)], axis=0) / (WINDOWS * DAYS)
    table = table.astype(np.float32)
    high = table.astype(jnp.bfloat16)
    low = (table - high.astype(np.float32)).astype(jnp.bfloat16)
    return high, low


def kernel(
    x_hbm, taper_hbm, tables_hbm, out_ref,
    x_ref, taper_ref, tables, head_f, send_m, send_t, recv_t, mix_f, send_e, recv_m, far,
    send_c, recv_d, lag_f, lag_rows, out_f,
    x_in, taper_in, tables_in,
    ready, t_send, t_recv, m_send, m_recv, e_send, f_send, f_recv, d_send, d_recv,
):
    c = lax.axis_index("chan")
    d = lax.axis_index("day")
    core = lax.rem(c, 2)
    chip = c // 2
    x = lax.rem(d, 4)
    y = d // 4

    x_copies = [
        pltpu.make_async_copy(
            x_hbm.at[0, pl.ds(4 * g, 4)], x_ref.at[pl.ds(4 * g, 4)], x_in.at[g]
        )
        for g in range(4)
    ]
    taper_copy = pltpu.make_async_copy(taper_hbm, taper_ref, taper_in)
    tables_copy = pltpu.make_async_copy(tables_hbm, tables, tables_in)
    x_copies[0].start()
    taper_copy.start()
    for g in range(1, 4):
        x_copies[g].start()
    tables_copy.start()

    barrier = pltpu.get_barrier_semaphore()
    for e in range(1, DAYS):
        pl.semaphore_signal(barrier, inc=1, device_id={"day": d ^ e}, device_id_type=MESH)
    for m in range(1, CHIPS):
        pl.semaphore_signal(barrier, inc=1, device_id={"chan": c ^ (2 * m)}, device_id_type=MESH)
    pl.semaphore_signal(barrier, inc=1, device_id={"chan": c ^ 1}, device_id_type=MESH)

    lane = lax.broadcasted_iota(jnp.int32, (1, 128), 1)
    group = lane // 32
    first16 = lax.rem(lane, 32) < 16
    sign64 = jnp.where(lane < 64, -1.0, 1.0).astype(F32)
    sign16 = jnp.where(first16, -1.0, 1.0).astype(F32)

    def swap16(v):
        return jnp.where(first16, pltpu.roll(v, 112, 1), pltpu.roll(v, 16, 1))

    def whiten(rows, partner):
        t = jnp.concatenate(rows, axis=0).T
        part = jnp.sum(t * t, axis=0, keepdims=True)
        power = (part + partner(part)) / BINS + 1e-06
        return t * taper_ref[...] * (1.0 / jnp.sqrt(power))

    taper_copy.wait()
    for g in range(4):
        x_copies[g].wait()
        rows = []
        for u in range(4):
            v = x_ref[4 * g + u, HEAD:, :].astype(F32)
            rows += [v[:, :128], v[:, 128:]]
        t = whiten(rows, swap16).astype(BF16)
        for n in range(4):
            send_t[n, g] = t[32 * n : 32 * n + 32]

    def whiten_heads(g, carry):
        for u in range(4):
            v = x_ref[4 * g + u, :HEAD, :].astype(F32)
            t = whiten([v[:, :128], v[:, 128:]], lambda part: pltpu.roll(part, 64, 1))
            head_f[pl.ds(4 * g + u, 128, stride=CH), :] = t
        return carry

    lax.fori_loop(0, 4, whiten_heads, 0)

    def pack(b, carry):
        part = head_f[pl.ds(pl.multiple_of(b * 128, 128), 128), :].astype(BF16)
        send_m[pl.ds(b * 8, 8)] = part.reshape(8, 16, 128)
        return carry

    lax.fori_loop(0, 16, pack, 0)

    pl.semaphore_wait(barrier, 23)
    for e in range(1, DAYS):
        pl.semaphore_signal(ready, inc=1, device_id={"day": d ^ e}, device_id_type=MESH)
    for n in range(1, 4):
        pltpu.make_async_remote_copy(
            send_t.at[x ^ n], recv_t.at[x], t_send, t_recv,
            device_id={"day": d ^ n}, device_id_type=MESH,
        ).start()
    recv_t[x] = send_t[x]

    pl.semaphore_wait(ready, 7)

    order = (0, 4, 1, 5, 2, 6, 3, 7)
    for e in order:
        to_day = d ^ e
        slot = lax.rem(to_day, 4) * 32 + (to_day // 4) * 16

        def send_head(m, carry, e=e, to_day=to_day, slot=slot):
            to = chip ^ m
            pltpu.make_async_remote_copy(
                send_m.at[slot + to], recv_m.at[core, d, chip], m_send, m_recv.at[e],
                device_id={"chan": to * 2 + core, "day": to_day}, device_id_type=MESH,
            ).start()
            return carry

        lax.fori_loop(1 if e == 0 else 0, CHIPS, send_head, 0)
    recv_m[core, d, chip] = send_m[x * 32 + y * 16 + chip]

    pltpu.make_async_copy(recv_t.at[pl.ds(0, 3)], recv_t.at[pl.ds(0, 3)], t_recv).wait()
    for g in range(4):
        tiles = [recv_t[n, g].astype(F32) for n in range(4)]
        for u in range(4):
            mixed = tiles[u]
            for n in range(4):
                if n != u:
                    mixed = jnp.where(group == n, pltpu.roll(tiles[n], (32 * (n - u)) % 128, 1), mixed)
            mix_f[pl.ds(4 * g + u, 32, stride=CH), :] = mixed
    send_e[...] = mix_f[...].astype(BF16).reshape(32, 16, 128)
    for h in range(2):
        to_day = d ^ (4 * h)
        slot = (y ^ h) * 16

        def send_tail(m, carry, h=h, to_day=to_day, slot=slot):
            to = chip ^ m
            pltpu.make_async_remote_copy(
                send_e.at[slot + to], recv_m.at[core, DAYS + y, chip], e_send, m_recv.at[DAYS + h],
                device_id={"chan": to * 2 + core, "day": to_day}, device_id_type=MESH,
            ).start()
            return carry

        lax.fori_loop(1 if h == 0 else 0, CHIPS, send_tail, 0)
    recv_m[core, DAYS + y, chip] = send_e[y * 16 + chip]

    def spread(side, k, tail):
        z = recv_m[side, k].reshape(256, 128)
        zf = z.astype(F32)
        turned = swap16(zf) * sign16 if tail else pltpu.roll(zf, 64, 1) * sign64
        turned = turned.astype(BF16)
        for n in range(DAYS):
            row = pl.multiple_of(n * 128 + side * 32, 32)
            far[k, pl.ds(row, 32), :] = z[32 * n : 32 * n + 32]
            far[k, pl.ds(row + 64, 32), :] = turned[32 * n : 32 * n + 32]

    blocks = [(e, d ^ e) for e in order] + [(DAYS + h, DAYS + (y ^ h)) for h in range(2)]

    def take_other(i, k):
        some = recv_m.at[1 - core, k]
        pltpu.make_async_copy(some, some, f_recv.at[i]).wait()
        spread(1 - core, k, i >= DAYS)

    last = None
    for i, k in blocks:
        some = recv_m.at[core, k]
        part = recv_m.at[core, k, pl.ds(0, 15)] if i in (0, DAYS) else some
        pltpu.make_async_copy(part, part, m_recv.at[i]).wait()
        pltpu.make_async_remote_copy(
            some, some, f_send, f_recv.at[i], device_id={"chan": c ^ 1}, device_id_type=MESH,
        ).start()
        spread(core, k, i >= DAYS)
        if last is not None:
            take_other(*last)
        last = (i, k)
    take_other(*last)

    near = jnp.concatenate([recv_m[core, k].reshape(256, 128) for k in range(KB)], axis=1)

    for s in range(4):
        p = (d // 2) ^ s
        rows = pl.ds(pl.multiple_of(p * 256, 256), 256)
        prod = lax.dot_general(
            near, jnp.concatenate([far[k, rows, :] for k in range(KB)], axis=1), NT,
            preferred_element_type=F32,
        )
        for e in range(2):
            send_c[2 * p + e] = prod[:, e * 128 : (e + 1) * 128].astype(BF16).reshape(CHIPS, 16, 128)

        def keep(day, to):
            pltpu.make_async_remote_copy(
                send_c.at[day, to], recv_d.at[d, chip], d_send, d_recv.at[d],
                device_id={"chan": to * 2 + core, "day": day}, device_id_type=MESH,
            ).start()

        def keep_both(m, carry):
            for e in range(2):
                keep(d ^ (2 * s + e), chip ^ m)
            return carry

        lax.fori_loop(1, CHIPS, keep_both, 0)
        keep(d ^ (2 * s + 1), chip)
        if s == 0:
            recv_d[d, chip] = send_c[d, chip]
        else:
            keep(d ^ (2 * s), chip)

    for e in range(DAYS):
        src = d ^ e
        some = recv_d.at[src] if e else recv_d.at[src, pl.ds(0, 15)]
        pltpu.make_async_copy(some, some, d_recv.at[src]).wait()
        lag_f[pl.ds(pl.multiple_of(src * 256, 256), 256), :] = (
            recv_d[src].reshape(256, 128).astype(F32)
        )

    tables_copy.wait()
    for n in range(4):
        for u in range(4):
            t = lag_f[pl.ds(n * 4 + u, 128, stride=16), :].T.astype(BF16)
            lag_rows[u * 64 : (u + 1) * 64, 0:128] = t[0:64]
            lag_rows[u * 64 : (u + 1) * 64, 128:256] = t[64:128]
        rows = lag_rows[...]
        lags = jnp.dot(rows, tables[0], preferred_element_type=F32)
        lags = lags + jnp.dot(rows, tables[1], preferred_element_type=F32)
        for u in range(4):
            for side in range(2):
                for b in range(2):
                    src = u * 64 + side * 32 + b * 16
                    dst = (b * 32 + side * 16) * 16 + n * 4 + u
                    for h in range(2):
                        out_f[h, pl.ds(dst, 16, stride=16), :] = (
                            lags[src : src + 16, h * 128 : (h + 1) * 128]
                        )
    for h in range(2):
        out_ref[:, h * 128 : (h + 1) * 128] = out_f[h]

    sent = send_t.at[pl.ds(0, 3)]
    pltpu.make_async_copy(sent, sent, t_send).wait()
    sent = send_m.at[pl.ds(0, 127)]
    pltpu.make_async_copy(sent, sent, m_send).wait()
    sent = send_e.at[pl.ds(0, 31)]
    pltpu.make_async_copy(sent, sent, e_send).wait()
    sent = recv_m.at[0]
    pltpu.make_async_copy(sent, sent, f_send).wait()
    sent = send_m.at[pl.ds(0, 127)]
    pltpu.make_async_copy(sent, sent, d_send).wait()


def shards(spectra):
    dma = pltpu.SemaphoreType.DMA
    out = pl.pallas_call(
        kernel,
        out_shape=jax.ShapeDtypeStruct((1024, 256), F32),
        in_specs=[pl.BlockSpec(memory_space=pltpu.HBM)] * 3,
        out_specs=pl.BlockSpec(memory_space=pltpu.VMEM),
        scratch_shapes=[
            pltpu.VMEM((CH, WINDOWS, 2 * BINS), BF16),
            pltpu.VMEM((BINS, 128), F32),
            pltpu.VMEM((2, LAGS, LAGS), BF16),
            pltpu.VMEM((2048, 128), F32),
            pltpu.VMEM((BINS, 16, 128), BF16),
            pltpu.VMEM((4, 4, 32, 128), BF16),
            pltpu.VMEM((4, 4, 32, 128), BF16),
            pltpu.VMEM((512, 128), F32),
            pltpu.VMEM((32, 16, 128), BF16),
            pltpu.VMEM((2, KB, CHIPS, 16, 128), BF16),
            pltpu.VMEM((KB, 1024, 128), BF16),
            pltpu.VMEM((DAYS, CHIPS, 16, 128), BF16),
            pltpu.VMEM((DAYS, CHIPS, 16, 128), BF16),
            pltpu.VMEM((2048, 128), F32),
            pltpu.VMEM((256, 256), BF16),
            pltpu.VMEM((2, 1024, 128), F32),
            dma((4,)),
            dma,
            dma,
            pltpu.SemaphoreType.REGULAR,
            dma,
            dma,
            dma,
            dma((KB,)),
            dma,
            dma,
            dma((KB,)),
            dma,
            dma((DAYS,)),
        ],
        compiler_params=pltpu.CompilerParams(
            collective_id=0, has_side_effects=True, vmem_limit_bytes=40 << 20
        ),
    )(*[
        pltpu.with_memory_space_constraint(v, pltpu.HBM)
        for v in (spectra, jnp.asarray(taper_table()), jnp.asarray(np.stack(lag_tables())))
    ])
    return out.reshape(64, 16, 256)


def solution(mesh):
    return jax.shard_map(
        shards,
        mesh=mesh,
        in_specs=(P("day", "chan", None, None),),
        out_specs=P("day", "chan", None),
        check_vma=False,
    )
```

time: 57.8 us -> 52.7 us (0.912)
  Pallas kernels: 55.4 us -> 51.7 us
  local copies, waits for them, and re-layouts: 2.26 us -> 0.97 us
    pallas_call x1, Pallas kernels: 55.4 us -> 51.7 us  [shards(): pl.pallas_call(kernel, out_shape=jax.ShapeDtypeStruct((1024, 256), F32),...]
    unnamed x1, local copies, waits for them, and re-layouts: 2.26 us -> 0.97 us
where the time goes in v3:
time: 52.7 us; the launch traced here: 52.6 us
  Pallas kernels  51.7 us (98%)
  local copies, waits for them, and re-layouts  0.97 us (2%)
    pallas_call x1, Pallas kernels, shards(): pl.pallas_call(kernel, out_shape=jax.ShapeDtypeStruct((1024, 256), F32),...  51.7 us

profile of v3, /device:TPU:1, one launch (start us, length us, event | category | flops | bytes accessed | tf_op | source)
XLA Modules:
  0.0 52.6 jit_solution(14153252080773623474)
XLA Ops:
  0.0 51.7 %shard_map.37 = f32[1024,256]{1,0:T(8,128)S(1)} custom-call(bf16[1,16,80,256]{3,2,1,0:T(8,128)(2,1)} %x_hbm.1, f32[128,128]{1,0:T(8,128)} %constant.4.clone.taper_hbm, bf16[2,256,256]{2,1,0:T(8,128)(2,1)} %constant.5.clone.tables_hbm), custom_call_target="tpu_custom_call" | custom-call | tf_op jit(solution)/shard_map/pallas_call | solution.py:276
  51.7 1.0 %copy.5 = f32[64,16,256]{2,1,0:T(8,128)} copy(f32[64,16,256]{2,1,0:T(8,128)S(1)} %bitcast.1) | data formatting | bytes 2097152

commit v4 on v3

v4 whole, which is shorter than its diff:
```python
import jax
import jax.numpy as jnp
import numpy as np
from jax import lax
from jax.experimental import pallas as pl
from jax.experimental.pallas import tpu as pltpu
from jax.sharding import PartitionSpec as P

F32 = jnp.float32
BF16 = jnp.bfloat16
MESH = pl.DeviceIdType.MESH
BINS = 128
LAGS = 256
WINDOWS = 80
CH = 16
DAYS = 8
CHIPS = 16
HEAD = 64
KB = 10
NT = (((1,), (1,)), ((), ()))


def taper_table():
    f = np.arange(BINS, dtype=np.float64)
    taper = 0.54 - 0.46 * np.cos(2.0 * np.pi * (f + 0.5) / BINS)
    return np.ascontiguousarray(np.broadcast_to(taper[:, None], (BINS, 128)).astype(np.float32))


def lag_tables():
    slot = np.arange(BINS)
    day = slot // CHIPS
    f = (day % 4) * 32 + (day // 4) * 16 + slot % CHIPS
    wound = (f[:, None] * (np.arange(LAGS)[None, :] - BINS)) % LAGS
    angle = 2.0 * np.pi / LAGS * wound
    table = np.concatenate([np.cos(angle), -np.sin(angle)], axis=0) / (WINDOWS * DAYS)
    table = table.astype(np.float32)
    high = table.astype(jnp.bfloat16)
    low = (table - high.astype(np.float32)).astype(jnp.bfloat16)
    return high, low


def kernel(
    x_hbm, taper_hbm, tables_hbm, out_ref,
    x_ref, taper_ref, tables, head_f, send_m, send_t, recv_t, mix_f, send_e, recv_m, far,
    send_c, recv_d, lag_f, lag_rows, out_f,
    x_in, taper_in, tables_in,
    ready, t_send, t_recv, m_send, m_recv, e_send, s_send, d_send, d_recv,
):
    c = lax.axis_index("chan")
    d = lax.axis_index("day")
    core = lax.rem(c, 2)
    z = lax.rem(c // 2, 8)
    y_hi = c // 16
    chip = z * 2 + y_hi
    x = lax.rem(d, 4)
    y = d // 4

    def chan_at(m):
        return c ^ (lax.rem(m, 2) * 16 + (m // 2) * 2)

    barrier = pltpu.get_barrier_semaphore()

    def greet_chan(to):
        pl.semaphore_signal(barrier, inc=1, device_id={"chan": to}, device_id_type=MESH)

    @pl.when(core == 0)
    def _():
        for m in range(CHIPS - 1, 0, -1):
            greet_chan(chan_at(m))
            greet_chan(chan_at(m) + 1)

    greet_chan(c ^ 1)
    for e in range(1, DAYS):
        pl.semaphore_signal(barrier, inc=1, device_id={"day": d ^ e}, device_id_type=MESH)

    x_copies = [
        pltpu.make_async_copy(
            x_hbm.at[0, pl.ds(4 * g, 4)], x_ref.at[pl.ds(4 * g, 4)], x_in.at[g]
        )
        for g in range(4)
    ]
    taper_copy = pltpu.make_async_copy(taper_hbm, taper_ref, taper_in)
    tables_copy = pltpu.make_async_copy(tables_hbm, tables, tables_in)
    x_copies[0].start()
    taper_copy.start()
    for g in range(1, 4):
        x_copies[g].start()
    tables_copy.start()

    lane = lax.broadcasted_iota(jnp.int32, (1, 128), 1)
    group = lane // 32
    first16 = lax.rem(lane, 32) < 16
    sign64 = jnp.where(lane < 64, -1.0, 1.0).astype(F32)
    sign16 = jnp.where(first16, -1.0, 1.0).astype(F32)

    def swap16(v):
        return jnp.where(first16, pltpu.roll(v, 112, 1), pltpu.roll(v, 16, 1))

    def whiten(rows, partner):
        t = jnp.concatenate(rows, axis=0).T
        part = jnp.sum(t * t, axis=0, keepdims=True)
        power = (part + partner(part)) / BINS + 1e-06
        return t * taper_ref[...] * (1.0 / jnp.sqrt(power))

    taper_copy.wait()
    for g in range(4):
        x_copies[g].wait()
        rows = []
        for u in range(4):
            v = x_ref[4 * g + u, HEAD:, :].astype(F32)
            rows += [v[:, :128], v[:, 128:]]
        t = whiten(rows, swap16).astype(BF16)
        for n in range(4):
            send_t[n, g] = t[32 * n : 32 * n + 32]

    def whiten_heads(g, carry):
        for u in range(4):
            v = x_ref[4 * g + u, :HEAD, :].astype(F32)
            t = whiten([v[:, :128], v[:, 128:]], lambda part: pltpu.roll(part, 64, 1))
            head_f[pl.ds(4 * g + u, 128, stride=CH), :] = t
        return carry

    lax.fori_loop(0, 4, whiten_heads, 0)

    def pack(b, carry):
        part = head_f[pl.ds(pl.multiple_of(b * 128, 128), 128), :].astype(BF16)
        send_m[pl.ds(b * 8, 8)] = part.reshape(8, 16, 128)
        return carry

    lax.fori_loop(0, 16, pack, 0)

    pl.semaphore_wait(barrier, 23)
    for e in range(1, DAYS):
        pl.semaphore_signal(ready, inc=1, device_id={"day": d ^ e}, device_id_type=MESH)
    for n in range(1, 4):
        pltpu.make_async_remote_copy(
            send_t.at[x ^ n], recv_t.at[x], t_send, t_recv,
            device_id={"day": d ^ n}, device_id_type=MESH,
        ).start()

    def send_head(e, m, sem):
        day = d ^ e
        slot = lax.rem(day, 4) * 32 + (day // 4) * 16 + (chip ^ m)
        pltpu.make_async_remote_copy(
            send_m.at[slot], recv_m.at[z, core, y_hi, d], m_send, sem,
            device_id={"chan": chan_at(m) - core, "day": day}, device_id_type=MESH,
        ).start()

    def send_same_day(r, carry):
        m = CHIPS - r
        send_head(0, m, m_recv.at[m // 2])
        return carry

    lax.fori_loop(1, CHIPS, send_same_day, 0)
    recv_t[x] = send_t[x]

    def keep_own(src, k):
        @pl.when(core == 0)
        def _():
            recv_m[z, 0, y_hi, k] = src[...]

        @pl.when(core == 1)
        def _():
            pltpu.make_async_remote_copy(
                src, recv_m.at[z, 1, y_hi, k], s_send, m_recv.at[0],
                device_id={"chan": c - 1}, device_id_type=MESH,
            ).start()

    keep_own(send_m.at[x * 32 + y * 16 + chip], d)

    pl.semaphore_wait(ready, 7)

    order = (4, 5, 7, 6, 3, 2, 1, 0)

    def send_heads(mz):
        def send(r, carry):
            send_head(DAYS - r // 2, 2 * mz + lax.rem(r, 2), m_recv.at[mz])
            return carry

        lax.fori_loop(2, 2 * DAYS, send, 0)

    def join_tails():
        pltpu.make_async_copy(recv_t.at[pl.ds(0, 3)], recv_t.at[pl.ds(0, 3)], t_recv).wait()
        for g in range(4):
            tiles = [recv_t[n, g].astype(F32) for n in range(4)]
            for u in range(4):
                mixed = tiles[u]
                for n in range(4):
                    if n != u:
                        moved = pltpu.roll(tiles[n], (32 * (n - u)) % 128, 1)
                        mixed = jnp.where(group == n, moved, mixed)
                mix_f[pl.ds(4 * g + u, 32, stride=CH), :] = mixed
        send_e[...] = mix_f[...].astype(BF16).reshape(32, 16, 128)
        keep_own(send_e.at[y * 16 + chip], DAYS + y)

    def send_tails(mz):
        def send(r, carry):
            h = r // 2
            m = 2 * mz + lax.rem(r, 2)
            pltpu.make_async_remote_copy(
                send_e.at[(y ^ h) * 16 + (chip ^ m)], recv_m.at[z, core, y_hi, DAYS + y],
                e_send, m_recv.at[mz],
                device_id={"chan": chan_at(m) - core, "day": d ^ (4 * h)}, device_id_type=MESH,
            ).start()
            return carry

        lax.fori_loop(0 if mz else 1, 4, send, 0)

    for mz in order[:4]:
        send_heads(mz)
    join_tails()
    for mz in order[:4]:
        send_tails(mz)
    for mz in order[4:]:
        send_heads(mz)
        send_tails(mz)

    def far_rows(p):
        for b in range(2):
            for side in range(2):
                for zz in range(2):
                    tiles = recv_m[lax.rem(p, 2) * 4 + 2 * b + zz, side, p // 2]
                    heads = tiles[:DAYS].reshape(DAYS * 16, 128).astype(F32)
                    tails = tiles[DAYS:].reshape(32, 128).astype(F32)
                    heads = (pltpu.roll(heads, 64, 1) * sign64).astype(BF16)
                    tails = (swap16(tails) * sign16).astype(BF16)
                    row = b * 128 + side * 32 + zz * 16
                    far[:, row : row + 16, :] = tiles
                    far[0:DAYS, row + 64 : row + 80, :] = heads.reshape(DAYS, 16, 128)
                    far[DAYS:KB, row + 64 : row + 80, :] = tails.reshape(2, 16, 128)

    def keep(e, m, side):
        day = d ^ e
        pltpu.make_async_remote_copy(
            send_c.at[day, side, chip ^ m], recv_d.at[d, chip], d_send, d_recv.at[e],
            device_id={"chan": chan_at(m) + side, "day": day}, device_id_type=MESH,
        ).start()

    @pl.when(core == 0)
    def _():
        for mz in order:
            some = recv_m.at[z ^ mz] if mz else send_m.at[pl.ds(0, 38)]
            pltpu.make_async_copy(some, some, m_recv.at[mz]).wait()

        for s in (1, 3, 2, 0):
            p = (d // 2) ^ s
            far_rows(p)
            for side in range(2):
                near = [recv_m[:, side, :, k].reshape(256, 128) for k in range(KB)]
                prod = lax.dot_general(
                    jnp.concatenate(near, axis=1),
                    jnp.concatenate([far[k] for k in range(KB)], axis=1),
                    NT, preferred_element_type=F32,
                ).astype(BF16)
                for b in range(2):
                    send_c[2 * p + b, side] = prod[:, b * 128 : (b + 1) * 128].reshape(CHIPS, 16, 128)

                def keep_all(r, carry, s=s, side=side):
                    keep(2 * s + lax.rem(r, 2), CHIPS - 1 - r // 2, side)
                    return carry

                lax.fori_loop(0, 2 * CHIPS - 2, keep_all, 0)
                keep(2 * s + 1, 0, side)
                if s or side:
                    keep(2 * s, 0, side)
                else:
                    recv_d[d, chip] = send_c[d, 0, chip]

    @pl.when(core == 0)
    def _():
        some = recv_d.at[d, pl.ds(0, 15)]
        pltpu.make_async_copy(some, some, d_recv.at[0]).wait()

    @pl.when(core == 1)
    def _():
        some = recv_d.at[d]
        pltpu.make_async_copy(some, some, d_recv.at[0]).wait()

    for e in range(DAYS):
        src = d ^ e
        if e:
            some = recv_d.at[src]
            pltpu.make_async_copy(some, some, d_recv.at[e]).wait()
        lag_f[pl.ds(pl.multiple_of(src * 256, 256), 256), :] = (
            recv_d[src].reshape(256, 128).astype(F32)
        )

    tables_copy.wait()
    for n in range(4):
        for u in range(4):
            t = lag_f[pl.ds(n * 4 + u, 128, stride=16), :].T.astype(BF16)
            lag_rows[u * 64 : (u + 1) * 64, 0:128] = t[0:64]
            lag_rows[u * 64 : (u + 1) * 64, 128:256] = t[64:128]
        rows = lag_rows[...]
        lags = jnp.dot(rows, tables[0], preferred_element_type=F32)
        lags = lags + jnp.dot(rows, tables[1], preferred_element_type=F32)
        for u in range(4):
            for side in range(2):
                for b in range(2):
                    src = u * 64 + side * 32 + b * 16
                    dst = (b * 32 + side * 16) * 16 + n * 4 + u
                    for h in range(2):
                        out_f[h, pl.ds(dst, 16, stride=16), :] = (
                            lags[src : src + 16, h * 128 : (h + 1) * 128]
                        )
    for h in range(2):
        out_ref[:, h * 128 : (h + 1) * 128] = out_f[h]

    sent = send_t.at[pl.ds(0, 3)]
    pltpu.make_async_copy(sent, sent, t_send).wait()
    sent = send_m.at[pl.ds(0, 127)]
    pltpu.make_async_copy(sent, sent, m_send).wait()
    sent = send_e.at[pl.ds(0, 31)]
    pltpu.make_async_copy(sent, sent, e_send).wait()

    @pl.when(core == 0)
    def _():
        some = send_c.reshape(256, 16, 128).at[pl.ds(0, 255)]
        pltpu.make_async_copy(some, some, d_send).wait()

    @pl.when(core == 1)
    def _():
        some = send_m.at[pl.ds(0, 2)]
        pltpu.make_async_copy(some, some, s_send).wait()


def shards(spectra):
    dma = pltpu.SemaphoreType.DMA
    out = pl.pallas_call(
        kernel,
        out_shape=jax.ShapeDtypeStruct((1024, 256), F32),
        in_specs=[pl.BlockSpec(memory_space=pltpu.HBM)] * 3,
        out_specs=pl.BlockSpec(memory_space=pltpu.VMEM),
        scratch_shapes=[
            pltpu.VMEM((CH, WINDOWS, 2 * BINS), BF16),
            pltpu.VMEM((BINS, 128), F32),
            pltpu.VMEM((2, LAGS, LAGS), BF16),
            pltpu.VMEM((2048, 128), F32),
            pltpu.VMEM((BINS, 16, 128), BF16),
            pltpu.VMEM((4, 4, 32, 128), BF16),
            pltpu.VMEM((4, 4, 32, 128), BF16),
            pltpu.VMEM((512, 128), F32),
            pltpu.VMEM((32, 16, 128), BF16),
            pltpu.VMEM((8, 2, 2, KB, 16, 128), BF16),
            pltpu.VMEM((KB, 256, 128), BF16),
            pltpu.VMEM((DAYS, 2, CHIPS, 16, 128), BF16),
            pltpu.VMEM((DAYS, CHIPS, 16, 128), BF16),
            pltpu.VMEM((2048, 128), F32),
            pltpu.VMEM((256, 256), BF16),
            pltpu.VMEM((2, 1024, 128), F32),
            dma((4,)),
            dma,
            dma,
            pltpu.SemaphoreType.REGULAR,
            dma,
            dma,
            dma,
            dma((8,)),
            dma,
            dma,
            dma,
            dma((DAYS,)),
        ],
        compiler_params=pltpu.CompilerParams(
            collective_id=0, has_side_effects=True, vmem_limit_bytes=40 << 20
        ),
    )(*[
        pltpu.with_memory_space_constraint(v, pltpu.HBM)
        for v in (spectra, jnp.asarray(taper_table()), jnp.asarray(np.stack(lag_tables())))
    ])
    return out.reshape(64, 16, 256)


def solution(mesh):
    return jax.shard_map(
        shards,
        mesh=mesh,
        in_specs=(P("day", "chan", None),),
        out_specs=P("day", "chan"),
        check_vma=False,
    )
```

time: 52.7 us -> 49.1 us (0.932)
  Pallas kernels: 51.7 us -> 48.1 us
    pallas_call x1, Pallas kernels: 51.7 us -> 48.1 us  [shards(): pl.pallas_call(kernel, out_shape=jax.ShapeDtypeStruct((1024, 256), F32),...]
where the time goes in v4:
time: 49.1 us; the launch traced here: 49 us
  Pallas kernels  48.1 us (98%)
  local copies, waits for them, and re-layouts  0.97 us (2%)
    pallas_call x1, Pallas kernels, shards(): pl.pallas_call(kernel, out_shape=jax.ShapeDtypeStruct((1024, 256), F32),...  48.1 us

profile of v4, /device:TPU:1, one launch (start us, length us, event | category | flops | bytes accessed | tf_op | source)
XLA Modules:
  0.0 49.0 jit_solution(5545675262670322146)
XLA Ops:
  0.0 48.1 %shard_map.37 = f32[1024,256]{1,0:T(8,128)S(1)} custom-call(bf16[1,16,80,256]{3,2,1,0:T(8,128)(2,1)} %x_hbm.1, f32[128,128]{1,0:T(8,128)} %constant.4.clone.taper_hbm, bf16[2,256,256]{2,1,0:T(8,128)(2,1)} %constant.5.clone.tables_hbm), custom_call_target="tpu_custom_call" | custom-call | tf_op jit(solution)/shard_map/pallas_call | solution.py:329
  48.1 1.0 %copy.5 = f32[64,16,256]{2,1,0:T(8,128)} copy(f32[64,16,256]{2,1,0:T(8,128)S(1)} %bitcast.1) | data formatting | bytes 2097152

commit v5 on v4

--- a/solution.py
+++ b/solution.py
@@ -206,13 +206,20 @@
 
         lax.fori_loop(0 if mz else 1, 4, send, 0)
 
-    for mz in order[:4]:
-        send_heads(mz)
+    def send_day(e):
+        def send(r, carry):
+            m = CHIPS - 1 - r
+            send_head(e, m, m_recv.at[m // 2])
+            return carry
+
+        lax.fori_loop(0, CHIPS, send, 0)
+
+    for e in (6, 2, 7, 3):
+        send_day(e)
     join_tails()
-    for mz in order[:4]:
-        send_tails(mz)
-    for mz in order[4:]:
-        send_heads(mz)
+    for e in (5, 1, 4):
+        send_day(e)
+    for mz in order:
         send_tails(mz)
 
     def far_rows(p):
@@ -245,7 +252,7 @@
         for s in (1, 3, 2, 0):
             p = (d // 2) ^ s
             far_rows(p)
-            for side in range(2):
+            for side in (1, 0):
                 near = [recv_m[:, side, :, k].reshape(256, 128) for k in range(KB)]
                 prod = lax.dot_general(
                     jnp.concatenate(near, axis=1),

time: 49.1 us -> 48 us (0.978); the launches traced: 49 us -> 47.2 us
  Pallas kernels: 48.1 us -> 46.2 us
    pallas_call x1, Pallas kernels: 48.1 us -> 46.2 us  [shards(): pl.pallas_call(kernel, out_shape=jax.ShapeDtypeStruct((1024, 256), F32),...]
where the time goes in v5:
time: 48 us; the launch traced here: 47.2 us
  Pallas kernels  46.2 us (96%)
  local copies, waits for them, and re-layouts  0.97 us (2%)
    pallas_call x1, Pallas kernels, shards(): pl.pallas_call(kernel, out_shape=jax.ShapeDtypeStruct((1024, 256), F32),...  46.2 us
    unnamed x1, local copies, waits for them, and re-layouts  0.97 us

profile of v5, /device:TPU:1, one launch (start us, length us, event | category | flops | bytes accessed | tf_op | source)
XLA Modules:
  0.0 47.2 jit_solution(17267271542268068481)
XLA Ops:
  0.0 46.2 %shard_map.37 = f32[1024,256]{1,0:T(8,128)S(1)} custom-call(bf16[1,16,80,256]{3,2,1,0:T(8,128)(2,1)} %x_hbm.1, f32[128,128]{1,0:T(8,128)} %constant.4.clone.taper_hbm, bf16[2,256,256]{2,1,0:T(8,128)(2,1)} %constant.5.clone.tables_hbm), custom_call_target="tpu_custom_call" | custom-call | tf_op jit(solution)/shard_map/pallas_call | solution.py:336
  46.2 1.0 %copy.5 = f32[64,16,256]{2,1,0:T(8,128)} copy(f32[64,16,256]{2,1,0:T(8,128)S(1)} %bitcast.1) | data formatting | bytes 2097152

commit v6 on v5

--- a/solution.py
+++ b/solution.py
@@ -65,13 +65,22 @@
 
     @pl.when(core == 0)
     def _():
-        for m in range(CHIPS - 1, 0, -1):
-            greet_chan(chan_at(m))
-            greet_chan(chan_at(m) + 1)
+        for mz in (4, 5, 7, 6, 3, 2, 1):
+            greet_chan(chan_at(2 * mz + 1))
+            greet_chan(chan_at(2 * mz))
+        greet_chan(chan_at(1))
+
+    for e in (6, 2, 7, 3, 5, 1, 4):
+        pl.semaphore_signal(barrier, inc=1, device_id={"day": d ^ e}, device_id_type=MESH)
+
+    @pl.when(core == 0)
+    def _():
+        for mz in (4, 5, 7, 6, 3, 2, 1):
+            greet_chan(chan_at(2 * mz + 1) + 1)
+            greet_chan(chan_at(2 * mz) + 1)
+        greet_chan(chan_at(1) + 1)
 
     greet_chan(c ^ 1)
-    for e in range(1, DAYS):
-        pl.semaphore_signal(barrier, inc=1, device_id={"day": d ^ e}, device_id_type=MESH)
 
     x_copies = [
         pltpu.make_async_copy(
@@ -97,7 +106,7 @@
         return jnp.where(first16, pltpu.roll(v, 112, 1), pltpu.roll(v, 16, 1))
 
     def whiten(rows, partner):
-        t = jnp.concatenate(rows, axis=0).T
+        t = jnp.concatenate(rows, axis=0).T.astype(F32)
         part = jnp.sum(t * t, axis=0, keepdims=True)
         power = (part + partner(part)) / BINS + 1e-06
         return t * taper_ref[...] * (1.0 / jnp.sqrt(power))
@@ -107,7 +116,7 @@
         x_copies[g].wait()
         rows = []
         for u in range(4):
-            v = x_ref[4 * g + u, HEAD:, :].astype(F32)
+            v = x_ref[4 * g + u, HEAD:, :]
             rows += [v[:, :128], v[:, 128:]]
         t = whiten(rows, swap16).astype(BF16)
         for n in range(4):
@@ -115,7 +124,7 @@
 
     def whiten_heads(g, carry):
         for u in range(4):
-            v = x_ref[4 * g + u, :HEAD, :].astype(F32)
+            v = x_ref[4 * g + u, :HEAD, :]
             t = whiten([v[:, :128], v[:, 128:]], lambda part: pltpu.roll(part, 64, 1))
             head_f[pl.ds(4 * g + u, 128, stride=CH), :] = t
         return carry
@@ -130,9 +139,9 @@
     lax.fori_loop(0, 16, pack, 0)
 
     pl.semaphore_wait(barrier, 23)
-    for e in range(1, DAYS):
+    for e in (6, 2, 7, 3, 5, 1, 4):
         pl.semaphore_signal(ready, inc=1, device_id={"day": d ^ e}, device_id_type=MESH)
-    for n in range(1, 4):
+    for n in (2, 1, 3):
         pltpu.make_async_remote_copy(
             send_t.at[x ^ n], recv_t.at[x], t_send, t_recv,
             device_id={"day": d ^ n}, device_id_type=MESH,
@@ -193,10 +202,14 @@
         send_e[...] = mix_f[...].astype(BF16).reshape(32, 16, 128)
         keep_own(send_e.at[y * 16 + chip], DAYS + y)
 
-    def send_tails(mz):
+    offsets = (4, 3, 5, 2, 6, 1, 7, 0)
+
+    def send_tails(kz):
+        mz = lax.rem(z + kz, 8) ^ z
+
         def send(r, carry):
-            h = r // 2
-            m = 2 * mz + lax.rem(r, 2)
+            h = 1 - r // 2
+            m = 2 * mz + 1 - lax.rem(r, 2)
             pltpu.make_async_remote_copy(
                 send_e.at[(y ^ h) * 16 + (chip ^ m)], recv_m.at[z, core, y_hi, DAYS + y],
                 e_send, m_recv.at[mz],
@@ -204,7 +217,7 @@
             ).start()
             return carry
 
-        lax.fori_loop(0 if mz else 1, 4, send, 0)
+        lax.fori_loop(0, 4 if kz else 3, send, 0)
 
     def send_day(e):
         def send(r, carry):
@@ -219,8 +232,8 @@
     join_tails()
     for e in (5, 1, 4):
         send_day(e)
-    for mz in order:
-        send_tails(mz)
+    for kz in offsets:
+        send_tails(kz)
 
     def far_rows(p):
         for b in range(2):
@@ -262,40 +275,48 @@
                 for b in range(2):
                     send_c[2 * p + b, side] = prod[:, b * 128 : (b + 1) * 128].reshape(CHIPS, 16, 128)
 
-                def keep_all(r, carry, s=s, side=side):
-                    keep(2 * s + lax.rem(r, 2), CHIPS - 1 - r // 2, side)
-                    return carry
-
-                lax.fori_loop(0, 2 * CHIPS - 2, keep_all, 0)
+                for mh in (1, 0):
+                    for kz in offsets:
+                        mz = lax.rem(z + kz, 8) ^ z
+
+                        def keep_all(r, carry, s=s, side=side, m=2 * mz + mh):
+                            keep(2 * s + 1 - r, m, side)
+                            return carry
+
+                        if kz or mh:
+                            lax.fori_loop(0, 2, keep_all, 0)
                 keep(2 * s + 1, 0, side)
                 if s or side:
                     keep(2 * s, 0, side)
                 else:
                     recv_d[d, chip] = send_c[d, 0, chip]
 
-    @pl.when(core == 0)
-    def _():
-        some = recv_d.at[d, pl.ds(0, 15)]
-        pltpu.make_async_copy(some, some, d_recv.at[0]).wait()
-
-    @pl.when(core == 1)
-    def _():
-        some = recv_d.at[d]
-        pltpu.make_async_copy(some, some, d_recv.at[0]).wait()
-
-    for e in range(DAYS):
-        src = d ^ e
-        if e:
-            some = recv_d.at[src]
-            pltpu.make_async_copy(some, some, d_recv.at[e]).wait()
+    def widen(src):
         lag_f[pl.ds(pl.multiple_of(src * 256, 256), 256), :] = (
             recv_d[src].reshape(256, 128).astype(F32)
         )
 
+    for e in (3, 2, 7, 6, 5, 4, 1):
+        some = recv_d.at[d ^ e]
+        pltpu.make_async_copy(some, some, d_recv.at[e]).wait()
+        widen(d ^ e)
+
+    @pl.when(core == 0)
+    def _():
+        some = recv_d.at[d, pl.ds(0, 15)]
+        pltpu.make_async_copy(some, some, d_recv.at[0]).wait()
+
+    @pl.when(core == 1)
+    def _():
+        some = recv_d.at[d]
+        pltpu.make_async_copy(some, some, d_recv.at[0]).wait()
+
+    widen(d)
+
     tables_copy.wait()
     for n in range(4):
         for u in range(4):
-            t = lag_f[pl.ds(n * 4 + u, 128, stride=16), :].T.astype(BF16)
+            t = lag_f[pl.ds(n * 4 + u, 128, stride=16), :].astype(BF16).T
             lag_rows[u * 64 : (u + 1) * 64, 0:128] = t[0:64]
             lag_rows[u * 64 : (u + 1) * 64, 128:256] = t[64:128]
         rows = lag_rows[...]

time: 48 us -> 47.4 us (0.987)
  no operation moved by 1% of the time
where the time goes in v6:
time: 47.4 us; the launch traced here: 46.9 us
  Pallas kernels  46 us (97%)
  local copies, waits for them, and re-layouts  0.97 us (2%)
    pallas_call x1, Pallas kernels, shards(): pl.pallas_call(kernel, out_shape=jax.ShapeDtypeStruct((1024, 256), F32),...  46 us
    unnamed x1, local copies, waits for them, and re-layouts  0.97 us

profile of v6, /device:TPU:1, one launch (start us, length us, event | category | flops | bytes accessed | tf_op | source)
XLA Modules:
  0.0 46.9 jit_solution(173870274086254027)
XLA Ops:
  0.0 46.0 %shard_map.37 = f32[1024,256]{1,0:T(8,128)S(1)} custom-call(bf16[1,16,80,256]{3,2,1,0:T(8,128)(2,1)} %x_hbm.1, f32[128,128]{1,0:T(8,128)} %constant.4.clone.taper_hbm, bf16[2,256,256]{2,1,0:T(8,128)(2,1)} %constant.5.clone.tables_hbm), custom_call_target="tpu_custom_call" | custom-call | tf_op jit(solution)/shard_map/pallas_call | solution.py:357
  46.0 1.0 %copy.5 = f32[64,16,256]{2,1,0:T(8,128)} copy(f32[64,16,256]{2,1,0:T(8,128)S(1)} %bitcast.1) | data formatting | bytes 2097152

commit v7 on v6

--- a/solution.py
+++ b/solution.py
@@ -220,12 +220,9 @@
         lax.fori_loop(0, 4 if kz else 3, send, 0)
 
     def send_day(e):
-        def send(r, carry):
-            m = CHIPS - 1 - r
-            send_head(e, m, m_recv.at[m // 2])
-            return carry
-
-        lax.fori_loop(0, CHIPS, send, 0)
+        for mh in (1, 0):
+            for kz in offsets:
+                send_head(e, 2 * (lax.rem(z + kz, 8) ^ z) + mh, m_recv.at[lax.rem(z + kz, 8) ^ z])
 
     for e in (6, 2, 7, 3):
         send_day(e)

time: 47.4 us -> 47.2 us (level)
  no operation moved by 1% of the time
where the time goes in v7:
time: 47.2 us; the launch traced here: 46.8 us
  Pallas kernels  45.8 us (97%)
  local copies, waits for them, and re-layouts  0.97 us (2%)
    pallas_call x1, Pallas kernels, shards(): pl.pallas_call(kernel, out_shape=jax.ShapeDtypeStruct((1024, 256), F32),...  45.8 us
    unnamed x1, local copies, waits for them, and re-layouts  0.97 us

profile of v7, /device:TPU:1, one launch (start us, length us, event | category | flops | bytes accessed | tf_op | source)
XLA Modules:
  0.0 46.8 jit_solution(556146340908831179)
XLA Ops:
  0.0 45.8 %shard_map.37 = f32[1024,256]{1,0:T(8,128)S(1)} custom-call(bf16[1,16,80,256]{3,2,1,0:T(8,128)(2,1)} %x_hbm.1, f32[128,128]{1,0:T(8,128)} %constant.4.clone.taper_hbm, bf16[2,256,256]{2,1,0:T(8,128)(2,1)} %constant.5.clone.tables_hbm), custom_call_target="tpu_custom_call" | custom-call | tf_op jit(solution)/shard_map/pallas_call | solution.py:354
  45.8 1.0 %copy.5 = f32[64,16,256]{2,1,0:T(8,128)} copy(f32[64,16,256]{2,1,0:T(8,128)S(1)} %bitcast.1) | data formatting | bytes 2097152

commit v8 on v7

--- a/solution.py
+++ b/solution.py
@@ -155,12 +155,12 @@
             device_id={"chan": chan_at(m) - core, "day": day}, device_id_type=MESH,
         ).start()
 
-    def send_same_day(r, carry):
-        m = CHIPS - r
-        send_head(0, m, m_recv.at[m // 2])
-        return carry
-
-    lax.fori_loop(1, CHIPS, send_same_day, 0)
+    for mh in (1, 0):
+        for kz in (4, 3, 5, 2, 6, 1, 7, 0):
+            if kz or mh:
+                mz = lax.rem(z + kz, 8) ^ z
+                send_head(0, 2 * mz + mh, m_recv.at[mz])
+
     recv_t[x] = send_t[x]
 
     def keep_own(src, k):

time: 47.2 us -> 47.2 us (level)
  no operation moved by 1% of the time
where the time goes in v8:
time: 47.2 us; the launch traced here: 46.8 us
  Pallas kernels  45.8 us (97%)
  local copies, waits for them, and re-layouts  0.97 us (2%)
    pallas_call x1, Pallas kernels, shards(): pl.pallas_call(kernel, out_shape=jax.ShapeDtypeStruct((1024, 256), F32),...  45.8 us
    unnamed x1, local copies, waits for them, and re-layouts  0.97 us

profile of v8, /device:TPU:1, one launch (start us, length us, event | category | flops | bytes accessed | tf_op | source)
XLA Modules:
  0.0 46.8 jit_solution(1596477475919823078)
XLA Ops:
  0.0 45.8 %shard_map.37 = f32[1024,256]{1,0:T(8,128)S(1)} custom-call(bf16[1,16,80,256]{3,2,1,0:T(8,128)(2,1)} %x_hbm.1, f32[128,128]{1,0:T(8,128)} %constant.4.clone.taper_hbm, bf16[2,256,256]{2,1,0:T(8,128)(2,1)} %constant.5.clone.tables_hbm), custom_call_target="tpu_custom_call" | custom-call | tf_op jit(solution)/shard_map/pallas_call | solution.py:354
  45.8 1.0 %copy.5 = f32[64,16,256]{2,1,0:T(8,128)} copy(f32[64,16,256]{2,1,0:T(8,128)S(1)} %bitcast.1) | data formatting | bytes 2097152
